TPU v7x, 512 devices: a whole 4x4x16 slice. The times are simulated.
512 devices in a mesh: gx: 8 (over y, core), gy: 4 (over z_hi), gz: 16 (over z_lo, x).
Axes of the slice: x: 4, y: 4, z: 16 (z_hi: 4, z_lo: 4; z = z_hi * 4 + z_lo), core: 2. Of those that a mesh axis runs over, the one named last changes fastest.
Arguments:
- inputs: bfloat16 [24576, 7168], P(('gy', 'gx'), 'gz'), may hold values from -6 to 6
- out_grads: bfloat16 [24576, 8192], P(('gy', 'gz'), 'gx'), may hold values from -0.0390625 to 0.0390625
- weights: bfloat16 [7168, 8192], P(('gz', 'gy'), 'gx'), may hold values from -0.29882812 to 0.29882812
- first_moment: float32 [7168, 8192], P(('gz', 'gy'), 'gx'), may hold values from -3 to 3
- second_moment: float32 [7168, 8192], P(('gz', 'gy'), 'gx'), may hold values from 0.05 to 2
Outputs:
- first_next: float32 [7168, 8192], P(('gz', 'gy'), 'gx')
- second_next: float32 [7168, 8192], P(('gz', 'gy'), 'gx')
- weight_next: bfloat16 [7168, 8192], P('gz', 'gx')
All inputs are finite; a program needn't handle non-finite values.
Results may differ from a plain program's by a relative error of at most 0.004.
Values may be sent and summed in bfloat16 or wider, within the bound.
A program may use at most 64 MiB of HBM per device.

v0:
```python
import jax
import jax.numpy as jnp
from jax import lax
from jax.sharding import PartitionSpec as P

beta_one = 0.9
beta_two = 0.95
adam_step = 10.0
learn_rate = 0.01
decay_rate = 0.1
epsilon = 1e-08


def contract(left, right):
    return lax.dot_general(
        left, right, (((0,), (0,)), ((), ())), preferred_element_type=jnp.float32
    )


def body(inputs, out_grads, weights, first_moment, second_moment):
    whole_inputs = lax.all_gather(inputs, "gx", axis=0, tiled=True)
    partial_grad = contract(whole_inputs, lax.all_gather(out_grads, "gz", axis=0, tiled=True))
    grad = lax.psum_scatter(
        partial_grad.astype(jnp.bfloat16), "gy", scatter_dimension=0, tiled=True
    ).astype(jnp.float32)
    first_next = beta_one * first_moment + (1.0 - beta_one) * grad
    second_next = beta_two * second_moment + (1.0 - beta_two) * grad * grad
    corr_one = 1.0 - beta_one**adam_step
    corr_two = 1.0 - beta_two**adam_step
    weight_wide = weights.astype(jnp.float32)
    update = (
        first_next / corr_one / (jnp.sqrt(second_next / corr_two) + epsilon)
        + decay_rate * weight_wide
    )
    owned_next = (weight_wide - learn_rate * update).astype(jnp.bfloat16)
    weight_next = lax.all_gather(owned_next, "gy", axis=0, tiled=True)
    return (first_next, second_next, weight_next)


def solution(mesh):
    in_specs = (
        P(("gy", "gx"), "gz"),
        P(("gy", "gz"), "gx"),
        P(("gz", "gy"), "gx"),
        P(("gz", "gy"), "gx"),
        P(("gz", "gy"), "gx"),
    )
    out_specs = (P(("gz", "gy"), "gx"), P(("gz", "gy"), "gx"), P("gz", "gx"))
    return jax.shard_map(body, mesh=mesh, in_specs=in_specs, out_specs=out_specs, check_vma=False)
```

profile of v0, /device:TPU:6, one launch (start us, length us, event | category | flops | bytes accessed | tf_op | source)
XLA Modules:
  0.0 320.1 jit_solution(8376757434707921580)
XLA Ops:
  7.2 0.0 all-gather.3.cloned.1.call-start
  7.2 0.7 all-gather.3.cloned.1.call-update
  7.9 0.0 all-gather.5.cloned.1.call-start
  7.9 0.7 all-gather.5.cloned.1.call-update
  8.6 0.0 copy-start
  8.7 0.0 copy-start.1
  8.7 0.0 copy-start.2
  8.7 0.0 reduce-scatter.2.cloned.1.call-start
  8.7 51.1 %all-gather.3.cloned.1.call-done = bf16[6144,448]{0,1:T(8,128)(2,1)} async-done(((bf16[768,448]{0,1:T(8,128)(2,1)}), bf16[6144,448]{0,1:T(8,128)(2,1)}) %all-gather.3.cloned.1.call-update) | async-done | bytes 5505040 | tf_op jit(solution)/shard_map/all_gather | solution.py:21
  59.9 147.7 %all-gather.5.cloned.1.call-done = bf16[6144,1024]{1,0:T(8,128)(2,1)} async-done(((bf16[384,1024]{1,0:T(8,128)(2,1)}), bf16[6144,1024]{1,0:T(8,128)(2,1)}) %all-gather.5.cloned.1.call-update) | async-done | bytes 12582928 | tf_op jit(solution)/shard_map/all_gather | solution.py:22
  207.6 12.2 %convolution_convert_fusion = bf16[448,1024]{1,0:T(8,128)(2,1)} fusion(bf16[6144,448]{0,1:T(8,128)(2,1)} %all-gather.3.cloned.1.call-done, bf16[6144,1024]{1,0:T(8,128)(2,1)} %all-gather.5.cloned.1.call-done), kind=kOutput, calls=%fused_computation | convolution fusion | flops 5637603328 | bytes 19005440 | tf_op jit(solution)/shard_map/dot_general | solution.py:15
  219.8 0.0 reduce-scatter.2.cloned.1.call-update
  219.8 57.0 %reduce-scatter.2.cloned.1.call-done = bf16[112,1024]{1,0:T(8,128)(2,1)} async-done(((bf16[448,1024]{1,0:T(8,128)(2,1)}), bf16[112,1024]{1,0:T(8,128)(2,1)}) %reduce-scatter.2.cloned.1.call-update) | async-done | bytes 229392 | tf_op jit(solution)/shard_map/reduce_scatter | solution.py:23
  276.8 0.0 copy-done
  276.8 0.0 copy-done.1
  276.8 0.0 copy-done.2
  276.8 2.2 fusion.3
  279.1 33.6 %all_gather.11 = bf16[448,1024]{1,0:T(8,128)(2,1)S(1)} all-gather(bf16[112,1024]{1,0:T(8,128)(2,1)S(1)} %get-tuple-element.3), channel_id=1, replica_groups=mesh['gx'=8,'gy'=4,'gz'=16] {'gy'}, dimensions={0}, use_global_device_ids=true | all-gather | bytes 1146880 | tf_op jit(solution)/shard_map/all_gather | solution.py:36
  312.7 0.9 copy.9
Async XLA Ops:
  7.2 52.7 %all-gather.3.cloned.1.call-start = ((), (), s32[]{:S(2)}) async-start(), calls=%async_computation.1 | async-start | bytes 6193152 | tf_op jit(solution)/shard_map/all_gather | solution.py:21
  7.9 199.7 %all-gather.5.cloned.1.call-start = ((), (), s32[]{:S(2)}) async-start(), calls=%async_computation.2 | async-start | bytes 13369344 | tf_op jit(solution)/shard_map/all_gather | solution.py:22
  8.6 268.2 %copy-start = (f32[112,1024]{1,0:T(8,128)S(1)}, f32[112,1024]{1,0:T(8,128)}, u32[]{:S(2)}) copy-start(f32[112,1024]{1,0:T(8,128)} %param.9) | copy-start | bytes 1376260
  8.7 268.2 %copy-start.1 = (f32[112,1024]{1,0:T(8,128)S(1)}, f32[112,1024]{1,0:T(8,128)}, u32[]{:S(2)}) copy-start(f32[112,1024]{1,0:T(8,128)} %param.8) | copy-start | bytes 1376260
  8.7 268.2 %copy-start.2 = (bf16[112,1024]{1,0:T(8,128)(2,1)S(1)}, bf16[112,1024]{1,0:T(8,128)(2,1)}, u32[]{:S(2)}) copy-start(bf16[112,1024]{1,0:T(8,128)(2,1)} %param.7) | copy-start | bytes 688132
  8.7 268.1 %reduce-scatter.2.cloned.1.call-start = ((), (), s32[]{:S(2)}) async-start(), calls=%async_computation.3 | async-start | bytes 1146880 | tf_op jit(solution)/shard_map/reduce_scatter | solution.py:23
Sparse Core Ops, SparseCore 0:
  10.1 49.7 all-gather.2
  62.0 145.6 all-gather.4
  220.0 56.8 reduce-scatter.1
where the time goes:
time: 324 us; the launch traced here: 320 us
  waiting for transfers between devices  257 us (79%)
  blocking collectives  33.6 us (10%)
  between operations  13.8 us (4%)
  matrix products  12.2 us (4%)
    all_gather x1, waiting for transfers between devices, body(): lax.all_gather(out_grads, 'gz', axis=0, tiled=True)  148 us
    reduce_scatter x1, waiting for transfers between devices, body(): lax.psum_scatter(partial_grad.astype(jnp.bfloat16), 'gy', scatter_dimensi...  57 us
    all_gather x1, waiting for transfers between devices, body(): whole_inputs = lax.all_gather(inputs, 'gx', axis=0, tiled=True)  51.1 us
    all_gather x1, blocking collectives, body(): weight_next = lax.all_gather(owned_next, 'gy', axis=0, tiled=True)  33.6 us
    dot_general x1, matrix products, contract(): lax.dot_general(left, right, (((0,), (0,)), ((), ())), preferred_element_...  12.2 us
  transfers between devices with their start and end apart: 3, of which 3 were waited for; matrix products, arithmetic and copies ran while one was open for 0% of the time, Pallas kernels for 0%

commit v1 on v0

v1 whole, which is shorter than its diff:
```python
import functools
import jax
import jax.numpy as jnp
from jax import lax
from jax.experimental import pallas as pl
from jax.experimental.pallas import tpu as pltpu
from jax.sharding import PartitionSpec as P

beta_one = 0.9
beta_two = 0.95
adam_step = 10.0
learn_rate = 0.01
decay_rate = 0.1
epsilon = 1e-08

BF = jnp.bfloat16
F32 = jnp.float32

RING = 16
ROWS = 112
HALF = 768
PART = 384
COLS = 1024
CHAINS = 4
WIDE = COLS // CHAINS


def kernel(a_ref, b_ref, w_ref, m1_ref, m2_ref, m1n_ref, m2n_ref, wn_ref,
           at_own, at_all, b_all, part, recv, send,
           a1_s, a1_r, loc, ym_s, yp_s, ym_r, yp_r, rm_s, rp_s, rm_r, rp_r,
           sib_s, sib_r, b_s, b_r, rs_s, rs_r, up_s, dn_s, up_r, dn_r, fw_s, fw_r):
    gx, h, gz = lax.axis_index("gx"), lax.axis_index("gy"), lax.axis_index("gz")
    y, c = gx // 2, gx % 2
    l, x = gz // 4, gz % 4
    z = 4 * h + l

    def dev(y_=y, c_=c, z_=z, x_=x):
        return {"gx": 2 * y_ + c_, "gy": z_ // 4, "gz": 4 * (z_ % 4) + x_}

    def remote(src, dst, s, r, to):
        return pltpu.make_async_remote_copy(
            src_ref=src, dst_ref=dst, send_sem=s, recv_sem=r,
            device_id=to, device_id_type=pl.DeviceIdType.MESH)

    y_up, y_dn, y_far = (y + 1) % 4, (y + 3) % 4, (y + 2) % 4
    z_up, z_dn = (z + 1) % RING, (z + RING - 1) % RING
    z_up4, z_dn4 = (z + 4) % RING, (z + RING - 4) % RING
    near = [dev(x_=(x + 1) % 4), dev(x_=(x + 3) % 4), dev(x_=(x + 2) % 4),
            dev(y_=y_up), dev(y_=y_dn), dev(c_=1 - c),
            dev(z_=z_up), dev(z_=z_dn), dev(z_=z_up4), dev(z_=z_dn4)]

    barrier = pltpu.get_barrier_semaphore()
    for to in near:
        pl.semaphore_signal(barrier, inc=1, device_id=to, device_id_type=pl.DeviceIdType.MESH)
    for i in range(4):
        @pl.when(jnp.logical_or(y != l, i != l))
        def _():
            pl.semaphore_signal(barrier, inc=1, device_id=dev(y_=l, z_=4 * h + i),
                                device_id_type=pl.DeviceIdType.MESH)
    at_own[...] = a_ref[...].T
    own_b = pltpu.make_async_copy(b_ref, b_all.at[x], loc.at[0])
    own_b.start()
    pl.semaphore_wait(barrier, len(near) + 4 - jnp.where(y == l, 1, 0))

    b_copies = [remote(b_ref, b_all.at[x], b_s.at[i], b_r.at[i], near[i]) for i in range(3)]
    a1 = [remote(at_own.at[pl.ds(ROWS * k, ROWS), :], at_all.at[l, k, c], a1_s.at[k], a1_r.at[l],
                 dev(y_=k, z_=4 * h + y)) for k in range(4)]
    stay = pltpu.make_async_copy(at_own.at[pl.ds(pl.multiple_of(ROWS * y, 16), ROWS), :],
                                 at_all.at[l, y, c], loc.at[1])
    for k in range(4):
        @pl.when(jnp.logical_or(y != l, k != y))
        def _():
            a1[k].start()

    @pl.when(y == l)
    def _():
        stay.start()
    for copy in b_copies:
        copy.start()

    order = [(l + 3) % 4, (l + 1) % 4, l, (l + 2) % 4]

    def hand_on(i, k):
        piece = at_all.at[i, k, c]
        return remote(piece, piece, sib_s.at[i, k], sib_r.at[i, k], dev(c_=1 - c))

    def to_up(i):
        piece = at_all.at[i, y, c]
        return remote(piece, piece, yp_s.at[i], yp_r.at[i], dev(y_=y_up))

    def to_dn(i):
        piece = at_all.at[i, y, c]
        return remote(piece, piece, ym_s.at[i], ym_r.at[i], dev(y_=y_dn))

    def relay_up(i, k):
        piece = at_all.at[i, k, c, :, pl.ds(0, HALF // 2)]
        return remote(piece, piece, rp_s.at[i], rp_r.at[i], dev(y_=y_up))

    def relay_dn(i, k):
        piece = at_all.at[i, k, c, :, pl.ds(HALF // 2, HALF // 2)]
        return remote(piece, piece, rm_s.at[i], rm_r.at[i], dev(y_=y_dn))

    for i in order:
        @pl.when(jnp.logical_or(y != l, i != l))
        def _():
            remote(at_all.at[i, y, c], at_all.at[i, y, c], a1_s.at[0], a1_r.at[i], near[0]).wait_recv()

        @pl.when(jnp.logical_and(y == l, i == l))
        def _():
            stay.wait()
        to_up(i).start()
        to_dn(i).start()
        hand_on(i, y).start()

    for i in order:
        remote(at_all.at[i, y_dn, c], at_all.at[i, y_dn, c], yp_s.at[i], yp_r.at[i], near[0]).wait_recv()
        relay_up(i, y_dn).start()
        hand_on(i, y_dn).start()
        remote(at_all.at[i, y_up, c], at_all.at[i, y_up, c], ym_s.at[i], ym_r.at[i], near[0]).wait_recv()
        relay_dn(i, y_up).start()
        hand_on(i, y_up).start()
    for i in order:
        relay_up(i, y_far).wait_recv()
        relay_dn(i, y_far).wait_recv()
        hand_on(i, y_far).start()

    own_b.wait()
    for i, q in enumerate([(x + 3) % 4, (x + 1) % 4, (x + 2) % 4]):
        remote(b_ref, b_all.at[q], b_s.at[i], b_r.at[i], near[i]).wait_recv()

    for i in order:
        for k in range(4):
            hand_on(i, k).wait_recv()

        @pl.loop(0, CHAINS)
        def _(j):
            cols = pl.ds(pl.multiple_of(j * WIDE, WIDE), WIDE)
            total = jnp.zeros((4 * ROWS, WIDE), F32)
            for core in range(2):
                left = at_all[i, :, core].reshape(4 * ROWS, HALF)
                right = b_all[pl.ds(2 * core, 2), :, cols].reshape(HALF, WIDE)
                total += jnp.dot(left, right, preferred_element_type=F32)
            part[i, :, :, cols] = total.reshape(4, ROWS, WIDE)

    def block(chain, s):
        d = (z + RING - 1 - s) % RING if chain < CHAINS // 2 else (z + 1 + s) % RING
        return part[d % 4, d // 4, :, pl.ds(chain * WIDE, WIDE)]

    def hop(chain, s):
        to = z_up if chain < CHAINS // 2 else z_dn
        return remote(send.at[chain, s], recv.at[chain, s], rs_s.at[chain, s], rs_r.at[chain, s], dev(z_=to))

    for chain in range(CHAINS):
        send[chain, 0] = block(chain, 0).astype(BF)
        hop(chain, 0).start()

    def ring_step(s, carry):
        for chain in range(CHAINS):
            mine = block(chain, s)
            hop(chain, s - 1).wait_recv()
            send[chain, s] = (mine + recv[chain, s - 1].astype(F32)).astype(BF)
            hop(chain, s).start()
        return carry

    lax.fori_loop(1, RING - 1, ring_step, 0)

    def weights_up(f):
        piece = wn_ref.at[h, :, pl.ds(f * WIDE, WIDE)]
        return remote(piece, piece, up_s.at[f], up_r.at[f], dev(z_=z_up4))

    def weights_dn(f):
        piece = wn_ref.at[h, :, pl.ds(f * WIDE, WIDE)]
        return remote(piece, piece, dn_s.at[f], dn_r.at[f], dev(z_=z_dn4))

    corr_one = 1.0 - beta_one**adam_step
    corr_two = 1.0 - beta_two**adam_step
    for chain in [0, 2, 1, 3]:
        cols = pl.ds(chain * WIDE, WIDE)
        mine = block(chain, RING - 1)
        hop(chain, RING - 2).wait_recv()
        grad = mine + recv[chain, RING - 2].astype(F32)
        first_next = beta_one * m1_ref[:, cols] + (1.0 - beta_one) * grad
        second_next = beta_two * m2_ref[:, cols] + (1.0 - beta_two) * grad * grad
        m1n_ref[:, cols] = first_next
        m2n_ref[:, cols] = second_next
        wide = w_ref[:, cols].astype(F32)
        update = (first_next / corr_one / (jnp.sqrt(second_next / corr_two) + epsilon)
                  + decay_rate * wide)
        wn_ref[h, :, cols] = (wide - learn_rate * update).astype(BF)
        weights_up(chain).start()
        weights_dn(chain).start()

    h_dn, h_up, h_far = (h + 3) % 4, (h + 1) % 4, (h + 2) % 4

    def pass_up(f, k):
        piece = wn_ref.at[k, :, pl.ds(f * WIDE, WIDE)]
        return remote(piece, piece, fw_s.at[f], fw_r.at[f], dev(z_=z_up4))

    def pass_dn(f, k):
        piece = wn_ref.at[k, :, pl.ds(f * WIDE, WIDE)]
        return remote(piece, piece, fw_s.at[f], fw_r.at[f], dev(z_=z_dn4))

    for f in [0, 2, 1, 3]:
        if f < CHAINS // 2:
            weights_up(f).wait_recv()
            pass_up(f, h_dn).start()
        else:
            weights_dn(f).wait_recv()
            pass_dn(f, h_up).start()
    for f in range(CHAINS):
        if f < CHAINS // 2:
            weights_dn(f).wait_recv()
        else:
            weights_up(f).wait_recv()
        pass_up(f, h_far).wait_recv()

    for copy in b_copies:
        copy.wait_send()
    for k in range(4):
        @pl.when(jnp.logical_or(y != l, k != y))
        def _():
            a1[k].wait_send()
    for i in range(4):
        to_up(i).wait_send()
        to_dn(i).wait_send()
        relay_up(i, 0).wait_send()
        relay_dn(i, 0).wait_send()
        for k in range(4):
            hand_on(i, k).wait_send()
    for chain in range(CHAINS):
        weights_up(chain).wait_send()
        weights_dn(chain).wait_send()
        pass_up(chain, 0).wait_send()

    def drain(s, carry):
        for chain in range(CHAINS):
            hop(chain, s).wait_send()
        return carry

    lax.fori_loop(0, RING - 1, drain, 0)


def body(inputs, out_grads, weights, first_moment, second_moment):
    vmem = pl.BlockSpec(memory_space=pltpu.VMEM)
    dma = pltpu.SemaphoreType.DMA
    own = first_moment.shape
    first_next, second_next, weight_next = pl.pallas_call(
        kernel,
        name="adam_grad",
        out_shape=(jax.ShapeDtypeStruct(own, F32), jax.ShapeDtypeStruct(own, F32),
                   jax.ShapeDtypeStruct((4, ROWS, COLS), BF)),
        in_specs=[vmem] * 5,
        out_specs=(vmem,) * 3,
        scratch_shapes=[
            pltpu.VMEM((4 * ROWS, HALF), BF),
            pltpu.VMEM((4, 4, 2, ROWS, HALF), BF),
            pltpu.VMEM((4, PART, COLS), BF),
            pltpu.VMEM((4, 4, ROWS, COLS), F32),
            pltpu.VMEM((CHAINS, RING - 1, ROWS, WIDE), BF),
            pltpu.VMEM((CHAINS, RING - 1, ROWS, WIDE), BF),
            dma((4,)), dma((4,)), dma((2,)),
            dma((4,)), dma((4,)), dma((4,)), dma((4,)),
            dma((4,)), dma((4,)), dma((4,)), dma((4,)),
            dma((4, 4)), dma((4, 4)),
            dma((3,)), dma((3,)),
            dma((CHAINS, RING - 1)), dma((CHAINS, RING - 1)),
            dma((CHAINS,)), dma((CHAINS,)), dma((CHAINS,)), dma((CHAINS,)),
            dma((CHAINS,)), dma((CHAINS,)),
        ],
        compiler_params=pltpu.CompilerParams(
            collective_id=0, has_side_effects=True, vmem_limit_bytes=48 * 2**20),
        cost_estimate=pl.CostEstimate(flops=5_700_000_000, bytes_accessed=6_000_000, transcendentals=0),
    )(inputs, out_grads, weights, first_moment, second_moment)
    return first_next, second_next, weight_next.reshape(4 * ROWS, COLS)


def solution(mesh):
    in_specs = (
        P(("gy", "gx"), "gz"),
        P(("gy", "gz"), "gx"),
        P(("gz", "gy"), "gx"),
        P(("gz", "gy"), "gx"),
        P(("gz", "gy"), "gx"),
    )
    out_specs = (P(("gz", "gy"), "gx"), P(("gz", "gy"), "gx"), P("gz", "gx"))
    return jax.shard_map(body, mesh=mesh, in_specs=in_specs, out_specs=out_specs, check_vma=False)
```

time: 324 us -> 185 us (0.57); the launches traced: 320 us -> 185 us
  waiting for transfers between devices: 257 us -> 0 us
  Pallas kernels: 0 us -> 179 us
  blocking collectives: 33.6 us -> 0 us
  between operations: 13.8 us -> 0.69 us
  matrix products: 12.2 us -> 0 us
  local copies, waits for them, and re-layouts: 0.94 us -> 5.03 us
    all_gather x2 -> x0, waiting for transfers between devices: 199 us -> none  [the longest x1 148 us: body(): lax.all_gather(out_grads, 'gz', axis=0, tiled=True)]
    pallas_call x0 -> x1, Pallas kernels: none -> 179 us  [body(): pl.pallas_call(kernel, name='adam_grad', out_shape=(jax.ShapeDtypeStruct(...]
    reduce_scatter x1 -> x0, waiting for transfers between devices: 57 us -> none  [body(): lax.psum_scatter(partial_grad.astype(jnp.bfloat16), 'gy', scatter_dimensi...]
    all_gather x1 -> x0, blocking collectives: 33.6 us -> none  [body(): weight_next = lax.all_gather(owned_next, 'gy', axis=0, tiled=True)]
    dot_general x1 -> x0, matrix products: 12.2 us -> none  [contract(): lax.dot_general(left, right, (((0,), (0,)), ((), ())), preferred_element_...]
    unnamed x7 -> x12, local copies, waits for them, and re-layouts: 0.94 us -> 5.03 us
  transfers between devices with their start and end apart: 3 -> 0, of which waited for: 3 -> 0; matrix products, arithmetic and copies ran while one was open for 0% -> 0% of each run, Pallas kernels for 0% -> 0%
where the time goes in v1:
time: 185 us
  Pallas kernels  179 us (97%)
  local copies, waits for them, and re-layouts  5.03 us (3%)
    pallas_call x1, Pallas kernels, body(): pl.pallas_call(kernel, name='adam_grad', out_shape=(jax.ShapeDtypeStruct(...  179 us
    unnamed x12, local copies, waits for them, and re-layouts  5.03 us

profile of v1, /device:TPU:6, one launch (start us, length us, event | category | flops | bytes accessed | tf_op | source)
XLA Modules:
  0.0 185.1 jit_solution(5928004378121594230)
XLA Ops:
  0.6 0.0 copy-start.1
  0.6 0.0 copy-start.3
  0.7 0.0 copy-start
  0.7 1.5 copy.8.a_ref
  2.1 0.0 copy-done.1
  2.2 0.0 copy-done.3
  2.2 0.1 copy-done
  2.2 0.0 copy-start.2
  2.2 1.0 copy-done.2
  3.2 179.4 %adam_grad.1 = (f32[112,1024]{1,0:T(8,128)S(1)}, f32[112,1024]{1,0:T(8,128)S(1)}, bf16[4,112,1024]{2,1,0:T(8,128)(2,1)S(1)}) custom-call(bf16[768,448]{1,0:T(8,128)(2,1)S(1)} %copy.8.a_ref, bf16[384,1024]{1,0:T(8,128)(2,1)S(1)} %copy-done, bf16[112,1024]{1,0:T(8,128)(2,1)S(1)} %copy-done.3, f32[112,1024]{1,0:T(8,128)S(1)} %copy-done.1, f32[112,1024]{1,0:T(8,128)S(1)} %copy-done.2), custom_call_target="tpu_custom_call" | custom-call | flops 5699999744 | bytes 6000000 | tf_op jit(solution)/shard_map/adam_grad/pallas_call | solution.py:247
  182.6 0.8 copy.12
  183.4 0.8 copy.13
  184.2 0.9 copy.14
Async XLA Ops:
  0.6 1.5 copy-start.1
  0.6 1.5 copy-start.3
  0.7 1.6 copy-start
  2.2 1.0 copy-start.2

commit v2 on v1

v2 whole, which is shorter than its diff:
```python
import functools
import jax
import jax.numpy as jnp
from jax import lax
from jax.experimental import pallas as pl
from jax.experimental.pallas import tpu as pltpu
from jax.sharding import PartitionSpec as P

beta_one = 0.9
beta_two = 0.95
adam_step = 10.0
learn_rate = 0.01
decay_rate = 0.1
epsilon = 1e-08

BF = jnp.bfloat16
F32 = jnp.float32

RING = 16
ROWS = 112
HALF = 768
PART = 384
COLS = 1024
CHAINS = 8
WIDE = COLS // CHAINS
SENDS = 4
TILE = 256


def kernel(a_ref, b_ref, w_ref, m1_ref, m2_ref, m1n_ref, m2n_ref, wn_ref,
           own, moved, at_all, b_all, part, recv, send,
           sc_s, sc_r, zm_s, zm_r, loc, ym_s, yp_s, ym_r, yp_r, rm_s, rp_s, rm_r, rp_r,
           sib_s, sib_r, b_s, b_r, rs_s, rs_r, up_s, dn_s, up_r, dn_r, fw_s, fw_r):
    gx, h, gz = lax.axis_index("gx"), lax.axis_index("gy"), lax.axis_index("gz")
    y, c = gx // 2, gx % 2
    l, x = gz // 4, gz % 4
    z = 4 * h + l

    def dev(y_=y, c_=c, z_=z, x_=x):
        return {"gx": 2 * y_ + c_, "gy": z_ // 4, "gz": 4 * (z_ % 4) + x_}

    def remote(src, dst, s, r, to):
        return pltpu.make_async_remote_copy(
            src_ref=src, dst_ref=dst, send_sem=s, recv_sem=r,
            device_id=to, device_id_type=pl.DeviceIdType.MESH)

    x_up, x_dn, x_far = (x + 1) % 4, (x + 3) % 4, (x + 2) % 4
    y_up, y_dn, y_far = (y + 1) % 4, (y + 3) % 4, (y + 2) % 4
    z_up, z_dn = (z + 1) % RING, (z + RING - 1) % RING
    z_up4, z_dn4 = (z + 4) % RING, (z + RING - 4) % RING
    near = [dev(x_=x_up), dev(x_=x_dn), dev(y_=y_up), dev(y_=y_dn), dev(y_=y_far), dev(c_=1 - c),
            dev(z_=z_up), dev(z_=z_dn), dev(z_=z_up4), dev(z_=z_dn4)]
    near += [dev(z_=4 * h + (l + i) % 4) for i in (1, 2, 3)]

    barrier = pltpu.get_barrier_semaphore()
    for to in near:
        pl.semaphore_signal(barrier, inc=1, device_id=to, device_id_type=pl.DeviceIdType.MESH)
    own[...] = a_ref[...].T.reshape(4, ROWS, HALF)
    own_b = pltpu.make_async_copy(b_ref, b_all.at[x], loc.at[0])
    own_b.start()
    pl.semaphore_wait(barrier, len(near))

    mine_at = pl.multiple_of(c * HALF, 128)

    def held(i, k, first=0, wide=HALF):
        return at_all.at[i, k, :, pl.ds(pl.multiple_of(mine_at + first, 128), wide)]

    def scatter(dk, stays):
        k = (y + dk) % 4
        return remote(own.at[k], held(l, k) if stays else moved.at[y], sc_s.at[dk - 1], sc_r.at[dk - 1], dev(y_=k))

    def z_move(i, src, p):
        return remote(src, held(l, y), zm_s.at[i], zm_r.at[l], dev(z_=4 * h + p))

    stay = pltpu.make_async_copy(own.at[y], held(l, y), loc.at[1])

    @pl.when(y == l)
    def _():
        stay.start()
        for dk in (1, 3, 2):
            scatter(dk, True).start()

    @pl.when(y != l)
    def _():
        z_move(0, own.at[y], y).start()
        for dk in (1, 3, 2):
            scatter(dk, False).start()

    def b_up():
        return remote(b_ref, b_all.at[x], b_s.at[0], b_r.at[0], dev(x_=x_up))

    def b_dn():
        return remote(b_ref, b_all.at[x], b_s.at[1], b_r.at[1], dev(x_=x_dn))

    def b_on_up(q):
        piece = b_all.at[q, pl.ds(0, PART // 2), :]
        return remote(piece, piece, b_s.at[2], b_r.at[2], dev(x_=x_up))

    def b_on_dn(q):
        piece = b_all.at[q, pl.ds(PART // 2, PART // 2), :]
        return remote(piece, piece, b_s.at[3], b_r.at[3], dev(x_=x_dn))

    b_up().start()
    b_dn().start()

    for dk in (1, 3, 2):
        p = (y + 4 - dk) % 4
        scatter(dk, False).wait_recv()

        @pl.when(p != l)
        def _():
            z_move(dk, moved.at[p], p).start()

    mirror = l // 2
    near_l = jnp.where(mirror == 1, 3 - l, l)
    order = [jnp.where(mirror == 1, 3 - i, i) for i in (near_l, 1 - near_l, 2, 3)]

    def hand_on(i, k):
        return remote(held(i, k), held(i, k), sib_s.at[i, k], sib_r.at[i, k], dev(c_=1 - c))

    def to_up(i):
        return remote(held(i, y), held(i, y), yp_s.at[i], yp_r.at[i], dev(y_=y_up))

    def to_dn(i):
        return remote(held(i, y), held(i, y), ym_s.at[i], ym_r.at[i], dev(y_=y_dn))

    def relay_up(i, k):
        piece = held(i, k, 0, HALF // 2)
        return remote(piece, piece, rp_s.at[i], rp_r.at[i], dev(y_=y_up))

    def relay_dn(i, k):
        piece = held(i, k, HALF // 2, HALF // 2)
        return remote(piece, piece, rm_s.at[i], rm_r.at[i], dev(y_=y_dn))

    def share(i):
        to_up(i).start()
        to_dn(i).start()
        hand_on(i, y).start()

    def relay(i):
        to_up(i).wait_recv()
        relay_up(i, y_dn).start()
        hand_on(i, y_dn).start()
        to_dn(i).wait_recv()
        relay_dn(i, y_up).start()
        hand_on(i, y_up).start()

    def far(i):
        relay_up(i, y_far).wait_recv()
        relay_dn(i, y_far).wait_recv()
        hand_on(i, y_far).start()

    @pl.when(y == l)
    def _():
        stay.wait()

    share(order[0])
    for n in (1, 2, 3):
        remote(own.at[0], held(order[n], y), zm_s.at[0], zm_r.at[order[n]], dev(c_=1 - c)).wait_recv()
        share(order[n])
        relay(order[n - 1])
        if n == 2:
            b_up().wait_recv()
            b_on_up(x_dn).start()
            b_dn().wait_recv()
            b_on_dn(x_up).start()
        if n >= 2:
            far(order[n - 2])
    relay(order[3])
    far(order[2])

    own_b.wait()
    b_on_up(x_far).wait_recv()
    b_on_dn(x_far).wait_recv()

    for n in range(4):
        i = order[n]
        if n == 1:
            far(order[3])
        for k in range(4):
            hand_on(i, k).wait_recv()

        @pl.loop(0, COLS // TILE)
        def _(j):
            cols = pl.ds(pl.multiple_of(j * TILE, TILE), TILE)
            total = jnp.dot(at_all[i].reshape(4 * ROWS, 2 * HALF), b_all[:, :, cols].reshape(2 * HALF, TILE),
                            preferred_element_type=F32)
            part[i, :, :, cols] = total.reshape(4, ROWS, TILE)

    def block(chain, s):
        d = (z + RING - 1 - s) % RING if chain < CHAINS // 2 else (z + 1 + s) % RING
        return part[d % 4, d // 4, :, pl.ds(chain * WIDE, WIDE)]

    def hop(chain, s):
        to = z_up if chain < CHAINS // 2 else z_dn
        return remote(send.at[chain, s], recv.at[chain, s], rs_s.at[chain, s], rs_r.at[chain, s], dev(z_=to))

    for chain in range(CHAINS):
        send[chain, 0] = block(chain, 0).astype(BF)
        hop(chain, 0).start()

    def ring_step(s, carry):
        for chain in range(CHAINS):
            mine = block(chain, s)
            hop(chain, s - 1).wait_recv()
            send[chain, s] = (mine + recv[chain, s - 1].astype(F32)).astype(BF)
            hop(chain, s).start()
        return carry

    lax.fori_loop(1, RING - 1, ring_step, 0)

    def weights(f, k):
        return wn_ref.at[k, :, pl.ds(f * (COLS // SENDS), COLS // SENDS)]

    def weights_up(f):
        return remote(weights(f, h), weights(f, h), up_s.at[f], up_r.at[f], dev(z_=z_up4))

    def weights_dn(f):
        return remote(weights(f, h), weights(f, h), dn_s.at[f], dn_r.at[f], dev(z_=z_dn4))

    corr_one = 1.0 - beta_one**adam_step
    corr_two = 1.0 - beta_two**adam_step
    for chain in [0, 1, 4, 5, 2, 3, 6, 7]:
        cols = pl.ds(chain * WIDE, WIDE)
        mine = block(chain, RING - 1)
        hop(chain, RING - 2).wait_recv()
        grad = mine + recv[chain, RING - 2].astype(F32)
        first_next = beta_one * m1_ref[:, cols] + (1.0 - beta_one) * grad
        second_next = beta_two * m2_ref[:, cols] + (1.0 - beta_two) * grad * grad
        m1n_ref[:, cols] = first_next
        m2n_ref[:, cols] = second_next
        wide = w_ref[:, cols].astype(F32)
        update = (first_next / corr_one / (jnp.sqrt(second_next / corr_two) + epsilon)
                  + decay_rate * wide)
        wn_ref[h, :, cols] = (wide - learn_rate * update).astype(BF)
        if chain % 2 == 1:
            weights_up(chain // 2).start()
            weights_dn(chain // 2).start()

    h_dn, h_up, h_far = (h + 3) % 4, (h + 1) % 4, (h + 2) % 4

    def pass_up(f, k):
        return remote(weights(f, k), weights(f, k), fw_s.at[f], fw_r.at[f], dev(z_=z_up4))

    def pass_dn(f, k):
        return remote(weights(f, k), weights(f, k), fw_s.at[f], fw_r.at[f], dev(z_=z_dn4))

    for f in [0, 2, 1, 3]:
        if f < SENDS // 2:
            weights_up(f).wait_recv()
            pass_up(f, h_dn).start()
        else:
            weights_dn(f).wait_recv()
            pass_dn(f, h_up).start()
    for f in range(SENDS):
        if f < SENDS // 2:
            weights_dn(f).wait_recv()
        else:
            weights_up(f).wait_recv()
        pass_up(f, h_far).wait_recv()

    b_up().wait_send()
    b_dn().wait_send()
    b_on_up(x_dn).wait_send()
    b_on_dn(x_up).wait_send()
    for dk in (1, 2, 3):
        scatter(dk, False).wait_send()

        @pl.when((y + 4 - dk) % 4 != l)
        def _():
            z_move(dk, moved.at[0], l).wait_send()

    @pl.when(y != l)
    def _():
        z_move(0, own.at[y], l).wait_send()
    for i in range(4):
        to_up(i).wait_send()
        to_dn(i).wait_send()
        relay_up(i, 0).wait_send()
        relay_dn(i, 0).wait_send()
        for k in range(4):
            hand_on(i, k).wait_send()
    for f in range(SENDS):
        weights_up(f).wait_send()
        weights_dn(f).wait_send()
        pass_up(f, 0).wait_send()

    def drain(s, carry):
        for chain in range(CHAINS):
            hop(chain, s).wait_send()
        return carry

    lax.fori_loop(0, RING - 1, drain, 0)


def body(inputs, out_grads, weights, first_moment, second_moment):
    vmem = pl.BlockSpec(memory_space=pltpu.VMEM)
    dma = pltpu.SemaphoreType.DMA
    own = first_moment.shape
    first_next, second_next, weight_next = pl.pallas_call(
        kernel,
        name="adam_grad",
        out_shape=(jax.ShapeDtypeStruct(own, F32), jax.ShapeDtypeStruct(own, F32),
                   jax.ShapeDtypeStruct((4, ROWS, COLS), BF)),
        in_specs=[vmem] * 5,
        out_specs=(vmem,) * 3,
        scratch_shapes=[
            pltpu.VMEM((4, ROWS, HALF), BF),
            pltpu.VMEM((4, ROWS, HALF), BF),
            pltpu.VMEM((4, 4, ROWS, 2 * HALF), BF),
            pltpu.VMEM((4, PART, COLS), BF),
            pltpu.VMEM((4, 4, ROWS, COLS), F32),
            pltpu.VMEM((CHAINS, RING - 1, ROWS, WIDE), BF),
            pltpu.VMEM((CHAINS, RING - 1, ROWS, WIDE), BF),
            dma((3,)), dma((3,)), dma((4,)), dma((4,)), dma((2,)),
            dma((4,)), dma((4,)), dma((4,)), dma((4,)),
            dma((4,)), dma((4,)), dma((4,)), dma((4,)),
            dma((4, 4)), dma((4, 4)),
            dma((4,)), dma((4,)),
            dma((CHAINS, RING - 1)), dma((CHAINS, RING - 1)),
            dma((SENDS,)), dma((SENDS,)), dma((SENDS,)), dma((SENDS,)),
            dma((SENDS,)), dma((SENDS,)),
        ],
        compiler_params=pltpu.CompilerParams(
            collective_id=0, has_side_effects=True, vmem_limit_bytes=48 * 2**20),
        cost_estimate=pl.CostEstimate(flops=5_700_000_000, bytes_accessed=6_000_000, transcendentals=0),
    )(inputs, out_grads, weights, first_moment, second_moment)
    return first_next, second_next, weight_next.reshape(4 * ROWS, COLS)


def solution(mesh):
    in_specs = (
        P(("gy", "gx"), "gz"),
        P(("gy", "gz"), "gx"),
        P(("gz", "gy"), "gx"),
        P(("gz", "gy"), "gx"),
        P(("gz", "gy"), "gx"),
    )
    out_specs = (P(("gz", "gy"), "gx"), P(("gz", "gy"), "gx"), P("gz", "gx"))
    return jax.shard_map(body, mesh=mesh, in_specs=in_specs, out_specs=out_specs, check_vma=False)
```

time: 185 us -> 151 us (0.82)
  Pallas kernels: 179 us -> 145 us
    pallas_call x1, Pallas kernels: 179 us -> 145 us  [body(): pl.pallas_call(kernel, name='adam_grad', out_shape=(jax.ShapeDtypeStruct(...]
where the time goes in v2:
time: 151 us; the launch traced here: 150 us
  Pallas kernels  145 us (96%)
  local copies, waits for them, and re-layouts  5.03 us (3%)
    pallas_call x1, Pallas kernels, body(): pl.pallas_call(kernel, name='adam_grad', out_shape=(jax.ShapeDtypeStruct(...  145 us
    unnamed x12, local copies, waits for them, and re-layouts  5.03 us

profile of v2, /device:TPU:6, one launch (start us, length us, event | category | flops | bytes accessed | tf_op | source)
XLA Modules:
  0.0 150.3 jit_solution(14530676860008405674)
XLA Ops:
  0.6 0.0 copy-start.1
  0.6 0.0 copy-start.3
  0.7 0.0 copy-start
  0.7 1.5 copy.8.a_ref
  2.1 0.0 copy-done.1
  2.2 0.0 copy-done.3
  2.2 0.1 copy-done
  2.2 0.0 copy-start.2
  2.2 1.0 copy-done.2
  3.2 144.5 %adam_grad.1 = (f32[112,1024]{1,0:T(8,128)S(1)}, f32[112,1024]{1,0:T(8,128)S(1)}, bf16[4,112,1024]{2,1,0:T(8,128)(2,1)S(1)}) custom-call(bf16[768,448]{1,0:T(8,128)(2,1)S(1)} %copy.8.a_ref, bf16[384,1024]{1,0:T(8,128)(2,1)S(1)} %copy-done, bf16[112,1024]{1,0:T(8,128)(2,1)S(1)} %copy-done.3, f32[112,1024]{1,0:T(8,128)S(1)} %copy-done.1, f32[112,1024]{1,0:T(8,128)S(1)} %copy-done.2), custom_call_target="tpu_custom_call" | custom-call | flops 5699999744 | bytes 6000000 | tf_op jit(solution)/shard_map/adam_grad/pallas_call | solution.py:300
  147.8 0.8 copy.12
  148.6 0.8 copy.13
  149.3 0.9 copy.14
Async XLA Ops:
  0.6 1.5 %copy-start.1 = (f32[112,1024]{1,0:T(8,128)S(1)}, f32[112,1024]{1,0:T(8,128)}, u32[]{:S(2)}) copy-start(f32[112,1024]{1,0:T(8,128)} %m1_ref.1) | copy-start | bytes 1376260
  0.6 1.5 %copy-start.3 = (bf16[112,1024]{1,0:T(8,128)(2,1)S(1)}, bf16[112,1024]{1,0:T(8,128)(2,1)}, u32[]{:S(2)}) copy-start(bf16[112,1024]{1,0:T(8,128)(2,1)} %w_ref.1) | copy-start | bytes 688132
  0.7 1.6 %copy-start = (bf16[384,1024]{1,0:T(8,128)(2,1)S(1)}, bf16[384,1024]{1,0:T(8,128)(2,1)}, u32[]{:S(2)}) copy-start(bf16[384,1024]{1,0:T(8,128)(2,1)} %b_ref.1) | copy-start | bytes 2359300
  2.2 1.0 copy-start.2

commit v3 on v2

v3 whole, which is shorter than its diff:
```python
import functools
import jax
import jax.numpy as jnp
from jax import lax
from jax.experimental import pallas as pl
from jax.experimental.pallas import tpu as pltpu
from jax.sharding import PartitionSpec as P

beta_one = 0.9
beta_two = 0.95
adam_step = 10.0
learn_rate = 0.01
decay_rate = 0.1
epsilon = 1e-08

BF = jnp.bfloat16
F32 = jnp.float32

RING = 16
ROWS = 112
HALF = 768
PART = 384
COLS = 1024
CHUNKS = 4
WIDE = COLS // CHUNKS
REACH = 8
TILE = 256


def kernel(a_ref, b_ref, w_ref, m1_ref, m2_ref, grad_ref, wn_ref,
           moved, at_all, b_all, part, recv, send, w_own, m1_own, m2_own,
           sc_s, sc_r, zm_s, zm_r, loc, ym_s, yp_s, ym_r, yp_r, rm_s, rp_s, rm_r, rp_r,
           sib_s, sib_r, b_s, b_r, rs_s, rs_r, up_s, dn_s, up_r, dn_r, fw_s, fw_r):
    gx, h, gz = lax.axis_index("gx"), lax.axis_index("gy"), lax.axis_index("gz")
    y, c = gx // 2, gx % 2
    l, x = gz // 4, gz % 4
    z = 4 * h + l

    def dev(y_=y, c_=c, z_=z, x_=x):
        return {"gx": 2 * y_ + c_, "gy": z_ // 4, "gz": 4 * (z_ % 4) + x_}

    def remote(src, dst, s, r, to):
        return pltpu.make_async_remote_copy(
            src_ref=src, dst_ref=dst, send_sem=s, recv_sem=r,
            device_id=to, device_id_type=pl.DeviceIdType.MESH)

    x_up, x_dn, x_far = (x + 1) % 4, (x + 3) % 4, (x + 2) % 4
    y_up, y_dn, y_far = (y + 1) % 4, (y + 3) % 4, (y + 2) % 4
    z_up, z_dn = (z + 1) % RING, (z + RING - 1) % RING
    z_up4, z_dn4 = (z + 4) % RING, (z + RING - 4) % RING
    near = [dev(x_=x_up), dev(x_=x_dn), dev(y_=y_up), dev(y_=y_dn), dev(y_=y_far), dev(c_=1 - c),
            dev(z_=z_up), dev(z_=z_dn), dev(z_=z_up4), dev(z_=z_dn4)]
    near += [dev(z_=4 * h + (l + i) % 4) for i in (1, 2, 3)]

    barrier = pltpu.get_barrier_semaphore()
    for to in near:
        pl.semaphore_signal(barrier, inc=1, device_id=to, device_id_type=pl.DeviceIdType.MESH)
    own_b = pltpu.make_async_copy(b_ref, b_all.at[x], loc.at[0])
    own_b.start()
    state = [pltpu.make_async_copy(src, dst, loc.at[2 + i])
             for i, (src, dst) in enumerate([(w_ref, w_own), (m1_ref, m1_own), (m2_ref, m2_own)])]
    for copy in state:
        copy.start()
    pl.semaphore_wait(barrier, len(near))

    mine_at = pl.multiple_of(c * HALF, 128)

    def own(k):
        return a_ref.at[pl.ds(pl.multiple_of(k * ROWS, 16), ROWS), :]

    def held(i, k, first=0, wide=HALF):
        return at_all.at[i, k, :, pl.ds(pl.multiple_of(mine_at + first, 128), wide)]

    def scatter(dk, stays):
        k = (y + dk) % 4
        return remote(own(k), held(l, k) if stays else moved.at[y], sc_s.at[dk - 1], sc_r.at[dk - 1], dev(y_=k))

    def z_move(i, src, p):
        return remote(src, held(l, y), zm_s.at[i], zm_r.at[l], dev(z_=4 * h + p))

    stay = pltpu.make_async_copy(own(y), held(l, y), loc.at[1])

    @pl.when(y == l)
    def _():
        stay.start()
        for dk in (1, 3, 2):
            scatter(dk, True).start()

    @pl.when(y != l)
    def _():
        z_move(0, own(y), y).start()
        for dk in (1, 3, 2):
            scatter(dk, False).start()

    def b_move(q, half, up, slot):
        piece = pl.ds(half * (PART // 2), PART // 2)
        src = b_all.at[q, piece, :] if slot == 2 else b_ref.at[piece, :]
        return remote(src, b_all.at[q, piece, :], b_s.at[slot, up], b_r.at[slot, up],
                      dev(x_=x_up if up else x_dn))

    for slot in (0, 1):
        for up in (1, 0):
            b_move(x, slot if up else 1 - slot, up, slot).start()

    for dk in (1, 3, 2):
        p = (y + 4 - dk) % 4
        scatter(dk, False).wait_recv()

        @pl.when(p != l)
        def _():
            z_move(dk, moved.at[p], p).start()

    mirror = l // 2
    near_l = jnp.where(mirror == 1, 3 - l, l)
    order = [jnp.where(mirror == 1, 3 - i, i) for i in (near_l, 1 - near_l, 2, 3)]

    def hand_on(i, k):
        return remote(held(i, k), held(i, k), sib_s.at[i, k], sib_r.at[i, k], dev(c_=1 - c))

    def to_up(i):
        return remote(held(i, y), held(i, y), yp_s.at[i], yp_r.at[i], dev(y_=y_up))

    def to_dn(i):
        return remote(held(i, y), held(i, y), ym_s.at[i], ym_r.at[i], dev(y_=y_dn))

    def relay_up(i, k):
        piece = held(i, k, 0, HALF // 2)
        return remote(piece, piece, rp_s.at[i], rp_r.at[i], dev(y_=y_up))

    def relay_dn(i, k):
        piece = held(i, k, HALF // 2, HALF // 2)
        return remote(piece, piece, rm_s.at[i], rm_r.at[i], dev(y_=y_dn))

    def share(i):
        to_up(i).start()
        to_dn(i).start()
        hand_on(i, y).start()

    def relay(i):
        to_up(i).wait_recv()
        relay_up(i, y_dn).start()
        hand_on(i, y_dn).start()
        to_dn(i).wait_recv()
        relay_dn(i, y_up).start()
        hand_on(i, y_up).start()

    def far(i):
        relay_up(i, y_far).wait_recv()
        relay_dn(i, y_far).wait_recv()
        hand_on(i, y_far).start()

    @pl.when(y == l)
    def _():
        stay.wait()

    share(order[0])
    for up, q in ((1, x_dn), (0, x_up)):
        b_move(q, 1 - up, up, 0).wait_recv()
        b_move(q, 1 - up, up, 2).start()
    for n in (1, 2, 3):
        remote(moved.at[0], held(order[n], y), zm_s.at[0], zm_r.at[order[n]], dev(c_=1 - c)).wait_recv()
        share(order[n])
        relay(order[n - 1])
        if n >= 2:
            far(order[n - 2])
    relay(order[3])

    own_b.wait()
    for up in (1, 0):
        for slot in (1, 2):
            b_move(x, 0, up, slot).wait_recv()

    def product(n):
        i = order[n]
        for k in range(4):
            hand_on(i, k).wait_recv()

        @pl.loop(0, COLS // TILE)
        def _(j):
            cols = pl.ds(pl.multiple_of(j * TILE, TILE), TILE)
            total = jnp.dot(at_all[i].reshape(4 * ROWS, 2 * HALF), b_all[:, :, cols].reshape(2 * HALF, TILE),
                            preferred_element_type=F32)
            part[i, :, :, cols] = total.reshape(4, ROWS, TILE)

    def term(up, f, e):
        d = (z + e) % RING if up else (z + RING - e) % RING
        return part[d % 4, d // 4, :, pl.ds(f * WIDE, WIDE)]

    def hop(up, f, e):
        return remote(send.at[up, f, e - 1], recv.at[up, f, e - 1], rs_s.at[up, f, e - 1], rs_r.at[up, f, e - 1],
                      dev(z_=z_up if up else z_dn))

    def far_side(up, f):
        return up == (1 if f < CHUNKS // 2 else 0)

    def first_hop(up, f, e):
        send[up, f, e - 1] = term(up, f, e).astype(BF)
        hop(up, f, e).start()

    def next_hop(up, f, e):
        mine = term(up, f, e)
        hop(up, f, e + 1).wait_recv()
        send[up, f, e - 1] = (mine + recv[up, f, e].astype(F32)).astype(BF)
        hop(up, f, e).start()

    ways = [(1, 0), (0, CHUNKS // 2), (1, 1), (0, CHUNKS // 2 + 1)]
    late = [(1, CHUNKS // 2), (0, 0), (1, CHUNKS // 2 + 1), (0, 1)]

    product(0)
    for up, f in ways:
        first_hop(up, f, REACH)
    far(order[2])
    product(1)
    far(order[3])
    product(2)
    product(3)
    for (up, f), (up_, f_) in zip(late, ways):
        first_hop(up, f, REACH - 1)
        next_hop(up_, f_, REACH - 1)

    def ring_step(i, carry):
        for up, f in ways + late:
            next_hop(up, f, REACH - 2 - i)
        return carry

    lax.fori_loop(0, REACH - 2, ring_step, 0)

    def weights(f, k):
        return wn_ref.at[k, :, pl.ds(f * (WIDE), WIDE)]

    def weights_up(f):
        return remote(weights(f, h), weights(f, h), up_s.at[f], up_r.at[f], dev(z_=z_up4))

    def weights_dn(f):
        return remote(weights(f, h), weights(f, h), dn_s.at[f], dn_r.at[f], dev(z_=z_dn4))

    corr_one = 1.0 - beta_one**adam_step
    corr_two = 1.0 - beta_two**adam_step
    for copy in state:
        copy.wait()
    for f in [0, 2, 1, 3]:
        cols = pl.ds(f * WIDE, WIDE)
        grad = term(1, f, 0)
        for up in (1, 0):
            hop(up, f, 1).wait_recv()
        grad = grad + recv[1, f, 0].astype(F32) + recv[0, f, 0].astype(F32)
        first_next = beta_one * m1_own[:, cols] + (1.0 - beta_one) * grad
        second_next = beta_two * m2_own[:, cols] + (1.0 - beta_two) * grad * grad
        grad_ref[:, cols] = grad
        wide = w_own[:, cols].astype(F32)
        update = (first_next / corr_one / (jnp.sqrt(second_next / corr_two) + epsilon)
                  + decay_rate * wide)
        wn_ref[h, :, cols] = (wide - learn_rate * update).astype(BF)
        weights_up(f).start()
        weights_dn(f).start()

    h_dn, h_up, h_far = (h + 3) % 4, (h + 1) % 4, (h + 2) % 4

    def pass_up(f, k):
        return remote(weights(f, k), weights(f, k), fw_s.at[f], fw_r.at[f], dev(z_=z_up4))

    def pass_dn(f, k):
        return remote(weights(f, k), weights(f, k), fw_s.at[f], fw_r.at[f], dev(z_=z_dn4))

    for f in [0, 2, 1, 3]:
        if f < CHUNKS // 2:
            weights_up(f).wait_recv()
            pass_up(f, h_dn).start()
        else:
            weights_dn(f).wait_recv()
            pass_dn(f, h_up).start()
    for f in range(CHUNKS):
        if f < CHUNKS // 2:
            weights_dn(f).wait_recv()
        else:
            weights_up(f).wait_recv()
        pass_up(f, h_far).wait_recv()

    for slot in (0, 1, 2):
        for up in (1, 0):
            b_move(x, 0, up, slot).wait_send()
    for dk in (1, 2, 3):
        scatter(dk, False).wait_send()

        @pl.when((y + 4 - dk) % 4 != l)
        def _():
            z_move(dk, moved.at[0], l).wait_send()

    @pl.when(y != l)
    def _():
        z_move(0, own(y), l).wait_send()
    for i in range(4):
        to_up(i).wait_send()
        to_dn(i).wait_send()
        relay_up(i, 0).wait_send()
        relay_dn(i, 0).wait_send()
        for k in range(4):
            hand_on(i, k).wait_send()
    for f in range(CHUNKS):
        weights_up(f).wait_send()
        weights_dn(f).wait_send()
        pass_up(f, 0).wait_send()

    for up, f in ways:
        hop(up, f, REACH).wait_send()

    def drain(i, carry):
        for up, f in ways + late:
            hop(up, f, i + 1).wait_send()
        return carry

    lax.fori_loop(0, REACH - 1, drain, 0)


def body(inputs, out_grads, weights, first_moment, second_moment):
    vmem = pl.BlockSpec(memory_space=pltpu.VMEM)
    dma = pltpu.SemaphoreType.DMA
    own = first_moment.shape
    grad, weight_next = pl.pallas_call(
        kernel,
        name="adam_grad",
        out_shape=(jax.ShapeDtypeStruct(own, F32),
                   jax.ShapeDtypeStruct((4, ROWS, COLS), BF)),
        in_specs=[pl.BlockSpec(memory_space=pltpu.HBM)] * 5,
        out_specs=(vmem,) * 2,
        scratch_shapes=[
            pltpu.VMEM((4, ROWS, HALF), BF),
            pltpu.VMEM((4, 4, ROWS, 2 * HALF), BF),
            pltpu.VMEM((4, PART, COLS), BF),
            pltpu.VMEM((4, 4, ROWS, COLS), F32),
            pltpu.VMEM((2, CHUNKS, REACH, ROWS, WIDE), BF),
            pltpu.VMEM((2, CHUNKS, REACH, ROWS, WIDE), BF),
            pltpu.VMEM((ROWS, COLS), BF),
            pltpu.VMEM((ROWS, COLS), F32),
            pltpu.VMEM((ROWS, COLS), F32),
            dma((3,)), dma((3,)), dma((4,)), dma((4,)), dma((5,)),
            dma((4,)), dma((4,)), dma((4,)), dma((4,)),
            dma((4,)), dma((4,)), dma((4,)), dma((4,)),
            dma((4, 4)), dma((4, 4)),
            dma((3, 2)), dma((3, 2)),
            dma((2, CHUNKS, REACH)), dma((2, CHUNKS, REACH)),
            dma((CHUNKS,)), dma((CHUNKS,)), dma((CHUNKS,)), dma((CHUNKS,)),
            dma((CHUNKS,)), dma((CHUNKS,)),
        ],
        compiler_params=pltpu.CompilerParams(
            collective_id=0, has_side_effects=True, vmem_limit_bytes=60 * 2**20),
        cost_estimate=pl.CostEstimate(flops=5_700_000_000, bytes_accessed=6_000_000, transcendentals=0),
    )(inputs.T, out_grads, weights, first_moment, second_moment)
    first_next = beta_one * first_moment + (1.0 - beta_one) * grad
    second_next = beta_two * second_moment + (1.0 - beta_two) * grad * grad
    return first_next, second_next, weight_next.reshape(4 * ROWS, COLS)


def solution(mesh):
    in_specs = (
        P(("gy", "gx"), "gz"),
        P(("gy", "gz"), "gx"),
        P(("gz", "gy"), "gx"),
        P(("gz", "gy"), "gx"),
        P(("gz", "gy"), "gx"),
    )
    out_specs = (P(("gz", "gy"), "gx"), P(("gz", "gy"), "gx"), P("gz", "gx"))
    return jax.shard_map(body, mesh=mesh, in_specs=in_specs, out_specs=out_specs, check_vma=False)
```

time: 151 us -> 136 us (0.901)
  Pallas kernels: 145 us -> 132 us
  local copies, waits for them, and re-layouts: 5.03 us -> 0.94 us
  other arithmetic: 0 us -> 2.22 us
    pallas_call x1, Pallas kernels: 145 us -> 132 us  [body(): pl.pallas_call(kernel, name='adam_grad', out_shape=(jax.ShapeDtypeStruct(...]
    unnamed x12 -> x7, local copies, waits for them, and re-layouts: 5.03 us -> 0.94 us
    add x0 -> x1, other arithmetic: none -> 2.22 us  [body(): second_next = beta_two * second_moment + (1.0 - beta_two) * grad * grad]
where the time goes in v3:
time: 136 us
  Pallas kernels  132 us (97%)
  other arithmetic  2.22 us (2%)
    pallas_call x1, Pallas kernels, body(): pl.pallas_call(kernel, name='adam_grad', out_shape=(jax.ShapeDtypeStruct(...  132 us

profile of v3, /device:TPU:6, one launch (start us, length us, event | category | flops | bytes accessed | tf_op | source)
XLA Modules:
  0.0 135.6 jit_solution(7405056451345386546)
XLA Ops:
  0.6 0.0 copy-start.1
  0.6 0.0 copy-start.2
  0.7 131.8 %adam_grad.1 = (f32[112,1024]{1,0:T(8,128)}, bf16[4,112,1024]{2,1,0:T(8,128)(2,1)}) custom-call(bf16[448,768]{1,0:T(8,128)(2,1)} %bitcast.3, bf16[384,1024]{1,0:T(8,128)(2,1)} %b_ref.1, bf16[112,1024]{1,0:T(8,128)(2,1)} %w_ref.1, f32[112,1024]{1,0:T(8,128)} %m1_ref.1, f32[112,1024]{1,0:T(8,128)} %m2_ref.1), custom_call_target="tpu_custom_call" | custom-call | flops 5699999744 | bytes 6000000 | tf_op jit(solution)/shard_map/adam_grad/pallas_call | solution.py:319
  132.4 0.0 copy-done.1
  132.5 0.0 copy-done.2
  132.5 0.0 copy-start
  132.5 2.2 %fusion = (f32[112,1024]{1,0:T(8,128)}, f32[112,1024]{1,0:T(8,128)}) fusion(f32[112,1024]{1,0:T(8,128)} %get-tuple-element.5, f32[112,1024]{1,0:T(8,128)S(1)} %copy-done.2, f32[112,1024]{1,0:T(8,128)S(1)} %copy-done.1), kind=kLoop, calls=%fused_computation.1 | loop fusion | flops 802816 | bytes 2293760 | tf_op jit(solution)/shard_map/add | solution.py:350
  134.7 0.0 copy-done
  134.7 0.9 copy.9
Async XLA Ops:
  0.6 131.8 %copy-start.1 = (f32[112,1024]{1,0:T(8,128)S(1)}, f32[112,1024]{1,0:T(8,128)}, u32[]{:S(2)}) copy-start(f32[112,1024]{1,0:T(8,128)} %m1_ref.1) | copy-start | bytes 1376260
  0.6 131.8 %copy-start.2 = (f32[112,1024]{1,0:T(8,128)S(1)}, f32[112,1024]{1,0:T(8,128)}, u32[]{:S(2)}) copy-start(f32[112,1024]{1,0:T(8,128)} %m2_ref.1) | copy-start | bytes 1376260
  132.5 2.2 %copy-start = (bf16[4,112,1024]{2,1,0:T(8,128)(2,1)S(1)}, bf16[4,112,1024]{2,1,0:T(8,128)(2,1)}, u32[]{:S(2)}) copy-start(bf16[4,112,1024]{2,1,0:T(8,128)(2,1)} %get-tuple-element.6) | copy-start | bytes 2752516

commit v4 on v3

v4 whole, which is shorter than its diff:
```python
import functools
import jax
import jax.numpy as jnp
from jax import lax
from jax.experimental import pallas as pl
from jax.experimental.pallas import tpu as pltpu
from jax.sharding import PartitionSpec as P

beta_one = 0.9
beta_two = 0.95
adam_step = 10.0
learn_rate = 0.01
decay_rate = 0.1
epsilon = 1e-08

BF = jnp.bfloat16
F32 = jnp.float32

RING = 16
ROWS = 112
PART = 384
COLS = 1024
CHUNKS = 4
WIDE = COLS // CHUNKS
REACH = 8
TILE = 512


def kernel(a_ref, b_ref, w_ref, m1_ref, m2_ref, grad_ref, wn_ref,
           moved, at_all, b_all, part, recv, send, w_own, m1_own, m2_own,
           sc_s, sc_r, zm_s, zm_r, loc, stay_s, up_y, dn_y, nb_r, rl_s, rl_r,
           sib_s, sib_r, b_s, b_r, rs_s, rs_r, up_s, dn_s, up_r, dn_r, fw_s, fw_r):
    gx, h, gz = lax.axis_index("gx"), lax.axis_index("gy"), lax.axis_index("gz")
    y, c = gx // 2, gx % 2
    l, x = gz // 4, gz % 4
    z = 4 * h + l

    def dev(y_=y, c_=c, z_=z, x_=x):
        return {"gx": 2 * y_ + c_, "gy": z_ // 4, "gz": 4 * (z_ % 4) + x_}

    def remote(src, dst, s, r, to):
        return pltpu.make_async_remote_copy(
            src_ref=src, dst_ref=dst, send_sem=s, recv_sem=r,
            device_id=to, device_id_type=pl.DeviceIdType.MESH)

    x_up, x_dn = (x + 1) % 4, (x + 3) % 4
    y_up, y_dn, y_far = (y + 1) % 4, (y + 3) % 4, (y + 2) % 4
    z_up, z_dn = (z + 1) % RING, (z + RING - 1) % RING
    z_up4, z_dn4 = (z + 4) % RING, (z + RING - 4) % RING
    near = [dev(x_=x_up), dev(x_=x_dn), dev(y_=y_up), dev(y_=y_dn), dev(y_=y_far), dev(c_=1 - c),
            dev(z_=z_up), dev(z_=z_dn), dev(z_=z_up4), dev(z_=z_dn4)]
    near += [dev(z_=4 * h + (l + i) % 4) for i in (1, 2, 3)]

    barrier = pltpu.get_barrier_semaphore()
    for to in near:
        pl.semaphore_signal(barrier, inc=1, device_id=to, device_id_type=pl.DeviceIdType.MESH)
    own_b = pltpu.make_async_copy(b_ref, b_all.at[x], loc.at[0])
    own_b.start()
    state = [pltpu.make_async_copy(src, dst, loc.at[1 + i])
             for i, (src, dst) in enumerate([(w_ref, w_own), (m1_ref, m1_own), (m2_ref, m2_own)])]
    for copy in state:
        copy.start()
    pl.semaphore_wait(barrier, len(near))

    def number(up, e):
        return 0 if e == REACH else RING - 1 if e == 0 else 1 + 2 * (REACH - 1 - e) + (0 if up else 1)

    def pick(i, values):
        return jnp.where(i == 0, values[0], jnp.where(i == 1, values[1], jnp.where(i == 2, values[2], values[3])))

    turn = (y + 4 - 2 * c) % 4
    owner = turn < 2
    upward = jnp.logical_or(turn == 1, turn == 2)
    side = turn % 2

    def lanes(q):
        return pl.ds(pl.multiple_of(q * PART, 128), PART)

    def piece(n, q):
        return at_all.at[n, :, lanes(q)]

    def source(off, p, j):
        k = ((4 * h + p + off + RING) % RING) // 4
        return a_ref.at[pl.ds(pl.multiple_of(k * ROWS, 16), ROWS), lanes(j)]

    home = [0, number(True, 4), number(False, 4), RING - 1]
    offsets = [pick((l + 4 - y) % 4, v) for v in ([8, -7, 6, 7], [4, 5, -6, -5], [-4, -3, 2, 3], [0, 1, -2, -1])]

    def scatter(i, j, stays):
        q = 2 * c + j
        return remote(source(offsets[i], y, j), piece(home[i], q) if stays else moved.at[y, i],
                      sc_s.at[i, j], sc_r.at[y, i], dev(y_=q))

    def stay(i):
        return pltpu.make_async_copy(source(offsets[i], y, side), piece(home[i], y), stay_s.at[i])

    for i in range(4):
        for j in range(2):
            @pl.when(jnp.logical_and(2 * c + j != y, y == l))
            def _():
                scatter(i, j, True).start()

            @pl.when(jnp.logical_and(2 * c + j != y, y != l))
            def _():
                scatter(i, j, False).start()

        @pl.when(jnp.logical_and(owner, y == l))
        def _():
            stay(i).start()

    rank = {(1, 7): 0, (0, 7): 0, (1, 6): 0, (0, 6): 1, (1, 5): 1, (0, 5): 1,
            (1, 3): 2, (0, 3): 2, (1, 2): 2, (0, 2): 3, (1, 1): 3, (0, 1): 3}

    def z_move(src, n, p):
        return remote(src, piece(n, y), zm_s.at[n], zm_r.at[n], dev(z_=4 * h + p))

    def scattered(p, i):
        return remote(moved.at[p, i], moved.at[p, i], sc_s.at[0, 0], sc_r.at[p, i], dev(c_=1 - c))

    def z_moves(*which):
        for up, e in which:
            n = number(up, e)
            p = (l + 8 - e) % 4 if up else (l + e) % 4

            @pl.when(jnp.logical_and(owner, p == y))
            def _():
                z_move(source(e if up else -e, p, side), n, p).start()

            @pl.when(jnp.logical_and(owner, p != y))
            def _():
                scattered(p, rank[up, e]).wait_recv()
                z_move(moved.at[p, rank[up, e]], n, p).start()

    def b_move(q, half, up, slot):
        piece = pl.ds(half * (PART // 2), PART // 2)
        src = b_all.at[q, piece, :] if slot == 2 else b_ref.at[piece, :]
        return remote(src, b_all.at[q, piece, :], b_s.at[slot, up], b_r.at[slot, up],
                      dev(x_=x_up if up else x_dn))

    for slot in (0, 1):
        for up in (1, 0):
            b_move(x, slot if up else 1 - slot, up, slot).start()

    def to_up(n):
        return remote(piece(n, y), piece(n, y), up_y.at[n], nb_r.at[n], dev(y_=y_up))

    def to_dn(n):
        return remote(piece(n, y), piece(n, y), dn_y.at[n], nb_r.at[n], dev(y_=y_dn))

    def from_near(n):
        return piece(n, 2 * c + 1 - side)

    def pass_along(n):
        return remote(from_near(n), from_near(n), rl_s.at[n], rl_r.at[n], dev(y_=y_up if n % 2 else y_dn))

    def passes(n):
        return upward if n % 2 else jnp.logical_not(upward)

    def hand_on(n, j):
        return remote(piece(n, 2 * c + j), piece(n, 2 * c + j), sib_s.at[n, j], sib_r.at[n, j], dev(c_=1 - c))

    def share(*blocks):
        for n in blocks:
            if n in home:
                i = home.index(n)

                @pl.when(jnp.logical_and(owner, y == l))
                def _():
                    stay(i).wait()

                @pl.when(jnp.logical_and(owner, y != l))
                def _():
                    remote(moved.at[0, 0], piece(n, y), sc_s.at[0, 0], sc_r.at[l, i], dev(c_=1 - c)).wait_recv()
            else:
                @pl.when(owner)
                def _():
                    z_move(moved.at[0, 0], n, l).wait_recv()

            @pl.when(owner)
            def _():
                to_up(n).start()
                to_dn(n).start()
                hand_on(n, side).start()

    def relay(*blocks):
        for n in blocks:
            remote(from_near(n), from_near(n), up_y.at[n], nb_r.at[n], dev(c_=1 - c)).wait_recv()

            @pl.when(passes(n))
            def _():
                pass_along(n).start()
            hand_on(n, 1 - side).start()

    def far(*blocks):
        for n in blocks:
            @pl.when(jnp.logical_not(owner))
            def _():
                remote(moved.at[0, 0], piece(n, 2 * c + side), rl_s.at[n], rl_r.at[n], dev(c_=1 - c)).wait_recv()
                hand_on(n, side).start()

    def product(*blocks):
        for n in blocks:
            for j in range(2):
                remote(moved.at[0, 0], piece(n, 2 - 2 * c + j), sib_s.at[n, j], sib_r.at[n, j], dev(c_=1 - c)).wait_recv()

            @pl.loop(0, COLS // TILE)
            def _(j):
                cols = pl.ds(pl.multiple_of(j * TILE, TILE), TILE)
                part[n, :, cols] = jnp.dot(at_all[n], b_all[:, :, cols].reshape(4 * PART, TILE),
                                           preferred_element_type=F32)

    def term(up, f, e):
        return part[number(up, e), :, pl.ds(f * WIDE, WIDE)]

    def hop(up, f, e):
        return remote(send.at[up, f, e - 1], recv.at[up, f, e - 1], rs_s.at[up, f, e - 1], rs_r.at[up, f, e - 1],
                      dev(z_=z_up if up else z_dn))

    def far_side(up, f):
        return up == (1 if f < CHUNKS // 2 else 0)

    def first_hop(up, f, e):
        send[up, f, e - 1] = term(up, f, e).astype(BF)
        hop(up, f, e).start()

    def next_hop(up, f, e):
        mine = term(up, f, e)
        hop(up, f, e + 1).wait_recv()
        send[up, f, e - 1] = (mine + recv[up, f, e].astype(F32)).astype(BF)
        hop(up, f, e).start()

    def hops(e):
        for f in (0, 2, 1, 3):
            for up in ((1, 0) if f < CHUNKS // 2 else (0, 1)):
                if e < REACH - 1 or (e == REACH - 1 and far_side(up, f)):
                    next_hop(up, f, e)
                elif e == REACH - 1 or far_side(up, f):
                    first_hop(up, f, e)

    z_moves((1, 7), (0, 7))
    share(0)
    z_moves((1, 6), (0, 6), (1, 5), (0, 5))
    relay(0)
    share(1, 2)
    for up, q in ((1, x_dn), (0, x_up)):
        b_move(q, 1 - up, up, 0).wait_recv()
        b_move(q, 1 - up, up, 2).start()
    far(0)
    relay(1, 2)
    share(3, 4)
    z_moves((1, 3), (0, 3))
    far(1, 2)
    relay(3, 4)
    share(5, 6)
    z_moves((1, 2), (0, 2), (1, 1), (0, 1))
    far(3, 4)
    relay(5, 6)
    share(7, 8)

    own_b.wait()
    for up in (1, 0):
        for slot in (1, 2):
            b_move(x, 0, up, slot).wait_recv()

    product(0)
    hops(8)
    far(5, 6)
    relay(7, 8)
    share(9, 10)
    product(1, 2)
    hops(7)
    far(7, 8)
    relay(9, 10)
    share(11, 12)
    product(3, 4)
    hops(6)
    far(9, 10)
    relay(11, 12)
    share(13, 14)
    product(5, 6)
    hops(5)
    far(11, 12)
    relay(13, 14)
    share(15)
    product(7, 8)
    hops(4)
    far(13, 14)
    relay(15)
    product(9, 10)
    hops(3)
    far(15)
    product(11, 12)
    hops(2)
    product(13, 14)
    hops(1)
    product(15)

    def weights(f, k):
        return wn_ref.at[k, :, pl.ds(f * (WIDE), WIDE)]

    def weights_up(f):
        return remote(weights(f, h), weights(f, h), up_s.at[f], up_r.at[f], dev(z_=z_up4))

    def weights_dn(f):
        return remote(weights(f, h), weights(f, h), dn_s.at[f], dn_r.at[f], dev(z_=z_dn4))

    corr_one = 1.0 - beta_one**adam_step
    corr_two = 1.0 - beta_two**adam_step
    for copy in state:
        copy.wait()
    for f in [0, 2, 1, 3]:
        cols = pl.ds(f * WIDE, WIDE)
        grad = term(1, f, 0)
        for up in (1, 0):
            hop(up, f, 1).wait_recv()
        grad = grad + recv[1, f, 0].astype(F32) + recv[0, f, 0].astype(F32)
        first_next = beta_one * m1_own[:, cols] + (1.0 - beta_one) * grad
        second_next = beta_two * m2_own[:, cols] + (1.0 - beta_two) * grad * grad
        grad_ref[:, cols] = grad
        wide = w_own[:, cols].astype(F32)
        update = (first_next / corr_one / (jnp.sqrt(second_next / corr_two) + epsilon)
                  + decay_rate * wide)
        wn_ref[h, :, cols] = (wide - learn_rate * update).astype(BF)
        weights_up(f).start()
        weights_dn(f).start()

    h_dn, h_up, h_far = (h + 3) % 4, (h + 1) % 4, (h + 2) % 4

    def pass_up(f, k):
        return remote(weights(f, k), weights(f, k), fw_s.at[f], fw_r.at[f], dev(z_=z_up4))

    def pass_dn(f, k):
        return remote(weights(f, k), weights(f, k), fw_s.at[f], fw_r.at[f], dev(z_=z_dn4))

    for f in [0, 2, 1, 3]:
        if f < CHUNKS // 2:
            weights_up(f).wait_recv()
            pass_up(f, h_dn).start()
        else:
            weights_dn(f).wait_recv()
            pass_dn(f, h_up).start()
    for f in range(CHUNKS):
        if f < CHUNKS // 2:
            weights_dn(f).wait_recv()
        else:
            weights_up(f).wait_recv()
        pass_up(f, h_far).wait_recv()

    for slot in (0, 1, 2):
        for up in (1, 0):
            b_move(x, 0, up, slot).wait_send()
    for i in range(4):
        for j in range(2):
            @pl.when(2 * c + j != y)
            def _():
                scatter(i, j, False).wait_send()

    @pl.when(owner)
    def _():
        for n in range(RING):
            if n not in home:
                z_move(moved.at[0, 0], n, l).wait_send()
    for n in range(RING):
        @pl.when(owner)
        def _():
            to_up(n).wait_send()
            to_dn(n).wait_send()

        @pl.when(passes(n))
        def _():
            pass_along(n).wait_send()
        for j in range(2):
            hand_on(n, j).wait_send()
    for f in range(CHUNKS):
        weights_up(f).wait_send()
        weights_dn(f).wait_send()
        pass_up(f, 0).wait_send()

    for e in range(1, REACH + 1):
        for f in range(CHUNKS):
            for up in (1, 0):
                if e < REACH or far_side(up, f):
                    hop(up, f, e).wait_send()


def body(inputs, out_grads, weights, first_moment, second_moment):
    vmem = pl.BlockSpec(memory_space=pltpu.VMEM)
    dma = pltpu.SemaphoreType.DMA
    own = first_moment.shape
    grad, weight_next = pl.pallas_call(
        kernel,
        name="adam_grad",
        out_shape=(jax.ShapeDtypeStruct(own, F32),
                   jax.ShapeDtypeStruct((4, ROWS, COLS), BF)),
        in_specs=[pl.BlockSpec(memory_space=pltpu.HBM)] * 5,
        out_specs=(vmem,) * 2,
        scratch_shapes=[
            pltpu.VMEM((4, 4, ROWS, PART), BF),
            pltpu.VMEM((RING, ROWS, 4 * PART), BF),
            pltpu.VMEM((4, PART, COLS), BF),
            pltpu.VMEM((RING, ROWS, COLS), F32),
            pltpu.VMEM((2, CHUNKS, REACH, ROWS, WIDE), BF),
            pltpu.VMEM((2, CHUNKS, REACH, ROWS, WIDE), BF),
            pltpu.VMEM((ROWS, COLS), BF),
            pltpu.VMEM((ROWS, COLS), F32),
            pltpu.VMEM((ROWS, COLS), F32),
            dma((4, 2)), dma((4, 4)), dma((RING,)), dma((RING,)), dma((4,)), dma((4,)),
            dma((RING,)), dma((RING,)), dma((RING,)), dma((RING,)), dma((RING,)),
            dma((RING, 2)), dma((RING, 2)),
            dma((3, 2)), dma((3, 2)),
            dma((2, CHUNKS, REACH)), dma((2, CHUNKS, REACH)),
            dma((CHUNKS,)), dma((CHUNKS,)), dma((CHUNKS,)), dma((CHUNKS,)),
            dma((CHUNKS,)), dma((CHUNKS,)),
        ],
        compiler_params=pltpu.CompilerParams(
            collective_id=0, has_side_effects=True, vmem_limit_bytes=60 * 2**20),
        cost_estimate=pl.CostEstimate(flops=5_700_000_000, bytes_accessed=6_000_000, transcendentals=0),
    )(inputs.T, out_grads, weights, first_moment, second_moment)
    first_next = beta_one * first_moment + (1.0 - beta_one) * grad
    second_next = beta_two * second_moment + (1.0 - beta_two) * grad * grad
    return first_next, second_next, weight_next.reshape(4 * ROWS, COLS)


def solution(mesh):
    in_specs = (
        P(("gy", "gx"), "gz"),
        P(("gy", "gz"), "gx"),
        P(("gz", "gy"), "gx"),
        P(("gz", "gy"), "gx"),
        P(("gz", "gy"), "gx"),
    )
    out_specs = (P(("gz", "gy"), "gx"), P(("gz", "gy"), "gx"), P("gz", "gx"))
    return jax.shard_map(body, mesh=mesh, in_specs=in_specs, out_specs=out_specs, check_vma=False)
```

time: 136 us -> 123 us (0.904)
  the two profiles are of different devices: /device:TPU:6 before, /device:TPU:26 now
where the time goes in v4:
time: 123 us
  Pallas kernels  119 us (97%)
  other arithmetic  2.22 us (2%)
    pallas_call x1, Pallas kernels, body(): pl.pallas_call(kernel, name='adam_grad', out_shape=(jax.ShapeDtypeStruct(...  119 us

profile of v4, /device:TPU:26, one launch (start us, length us, event | category | flops | bytes accessed | tf_op | source)
XLA Modules:
  0.0 123.1 jit_solution(17605222312040880560)
XLA Ops:
  0.6 0.0 copy-start.1
  0.6 0.0 copy-start.2
  0.7 119.3 %adam_grad.1 = (f32[112,1024]{1,0:T(8,128)}, bf16[4,112,1024]{2,1,0:T(8,128)(2,1)}) custom-call(bf16[448,768]{1,0:T(8,128)(2,1)} %bitcast.3, bf16[384,1024]{1,0:T(8,128)(2,1)} %b_ref.1, bf16[112,1024]{1,0:T(8,128)(2,1)} %w_ref.1, f32[112,1024]{1,0:T(8,128)} %m1_ref.1, f32[112,1024]{1,0:T(8,128)} %m2_ref.1), custom_call_target="tpu_custom_call" | custom-call | flops 5699999744 | bytes 6000000 | tf_op jit(solution)/shard_map/adam_grad/pallas_call | solution.py:390
  119.9 0.0 copy-done.1
  119.9 0.0 copy-done.2
  119.9 0.0 copy-start
  119.9 2.2 %fusion = (f32[112,1024]{1,0:T(8,128)}, f32[112,1024]{1,0:T(8,128)}) fusion(f32[112,1024]{1,0:T(8,128)} %get-tuple-element.5, f32[112,1024]{1,0:T(8,128)S(1)} %copy-done.2, f32[112,1024]{1,0:T(8,128)S(1)} %copy-done.1), kind=kLoop, calls=%fused_computation.1 | loop fusion | flops 802816 | bytes 2293760 | tf_op jit(solution)/shard_map/add | solution.py:420
  122.2 0.0 copy-done
  122.2 0.9 copy.9
Async XLA Ops:
  0.6 119.3 %copy-start.1 = (f32[112,1024]{1,0:T(8,128)S(1)}, f32[112,1024]{1,0:T(8,128)}, u32[]{:S(2)}) copy-start(f32[112,1024]{1,0:T(8,128)} %m1_ref.1) | copy-start | bytes 1376260
  0.6 119.3 %copy-start.2 = (f32[112,1024]{1,0:T(8,128)S(1)}, f32[112,1024]{1,0:T(8,128)}, u32[]{:S(2)}) copy-start(f32[112,1024]{1,0:T(8,128)} %m2_ref.1) | copy-start | bytes 1376260
  119.9 2.2 %copy-start = (bf16[4,112,1024]{2,1,0:T(8,128)(2,1)S(1)}, bf16[4,112,1024]{2,1,0:T(8,128)(2,1)}, u32[]{:S(2)}) copy-start(bf16[4,112,1024]{2,1,0:T(8,128)(2,1)} %get-tuple-element.6) | copy-start | bytes 2752516

commit v5 on v4

--- a/solution.py
+++ b/solution.py
@@ -240,22 +240,24 @@
     z_moves((1, 7), (0, 7))
     share(0)
     z_moves((1, 6), (0, 6), (1, 5), (0, 5))
+    share(1, 2)
     relay(0)
-    share(1, 2)
     for up, q in ((1, x_dn), (0, x_up)):
         b_move(q, 1 - up, up, 0).wait_recv()
         b_move(q, 1 - up, up, 2).start()
+    share(3, 4)
+    relay(1, 2)
     far(0)
-    relay(1, 2)
-    share(3, 4)
-    z_moves((1, 3), (0, 3))
+    z_moves((1, 3), (0, 3), (1, 2), (0, 2), (1, 1), (0, 1))
+    share(5, 6)
+    relay(3, 4)
     far(1, 2)
-    relay(3, 4)
-    share(5, 6)
-    z_moves((1, 2), (0, 2), (1, 1), (0, 1))
+    share(7, 8)
+    relay(5, 6)
     far(3, 4)
-    relay(5, 6)
-    share(7, 8)
+    share(9, 10)
+    relay(7, 8)
+    far(5, 6)
 
     own_b.wait()
     for up in (1, 0):
@@ -264,31 +266,25 @@
 
     product(0)
     hops(8)
-    far(5, 6)
-    relay(7, 8)
-    share(9, 10)
+    share(11, 12)
+    relay(9, 10)
+    far(7, 8)
     product(1, 2)
     hops(7)
-    far(7, 8)
-    relay(9, 10)
-    share(11, 12)
+    share(13, 14, 15)
+    relay(11, 12)
+    far(9, 10)
     product(3, 4)
     hops(6)
-    far(9, 10)
-    relay(11, 12)
-    share(13, 14)
+    relay(13, 14, 15)
+    far(11, 12)
     product(5, 6)
     hops(5)
-    far(11, 12)
-    relay(13, 14)
-    share(15)
+    far(13, 14, 15)
     product(7, 8)
     hops(4)
-    far(13, 14)
-    relay(15)
     product(9, 10)
     hops(3)
-    far(15)
     product(11, 12)
     hops(2)
     product(13, 14)
@@ -321,8 +317,9 @@
         update = (first_next / corr_one / (jnp.sqrt(second_next / corr_two) + epsilon)
                   + decay_rate * wide)
         wn_ref[h, :, cols] = (wide - learn_rate * update).astype(BF)
-        weights_up(f).start()
-        weights_dn(f).start()
+        (weights_up if f < CHUNKS // 2 else weights_dn)(f).start()
+    for f in [0, 2, 1, 3]:
+        (weights_dn if f < CHUNKS // 2 else weights_up)(f).start()
 
     h_dn, h_up, h_far = (h + 3) % 4, (h + 1) % 4, (h + 2) % 4
 

time: 123 us -> 121 us (0.984)
  the two profiles are of different devices: /device:TPU:26 before, /device:TPU:6 now
where the time goes in v5:
time: 121 us; the launch traced here: 120 us
  Pallas kernels  116 us (96%)
  other arithmetic  2.22 us (2%)
    pallas_call x1, Pallas kernels, body(): pl.pallas_call(kernel, name='adam_grad', out_shape=(jax.ShapeDtypeStruct(...  116 us

profile of v5, /device:TPU:6, one launch (start us, length us, event | category | flops | bytes accessed | tf_op | source)
XLA Modules:
  0.0 119.5 jit_solution(14299595171382771143)
XLA Ops:
  0.6 0.0 copy-start.1
  0.6 0.0 copy-start.2
  0.7 115.7 %adam_grad.1 = (f32[112,1024]{1,0:T(8,128)}, bf16[4,112,1024]{2,1,0:T(8,128)(2,1)}) custom-call(bf16[448,768]{1,0:T(8,128)(2,1)} %bitcast.3, bf16[384,1024]{1,0:T(8,128)(2,1)} %b_ref.1, bf16[112,1024]{1,0:T(8,128)(2,1)} %w_ref.1, f32[112,1024]{1,0:T(8,128)} %m1_ref.1, f32[112,1024]{1,0:T(8,128)} %m2_ref.1), custom_call_target="tpu_custom_call" | custom-call | flops 5699999744 | bytes 6000000 | tf_op jit(solution)/shard_map/adam_grad/pallas_call | solution.py:387
  116.4 0.0 copy-done.1
  116.4 0.0 copy-done.2
  116.4 0.0 copy-start
  116.4 2.2 %fusion = (f32[112,1024]{1,0:T(8,128)}, f32[112,1024]{1,0:T(8,128)}) fusion(f32[112,1024]{1,0:T(8,128)} %get-tuple-element.5, f32[112,1024]{1,0:T(8,128)S(1)} %copy-done.2, f32[112,1024]{1,0:T(8,128)S(1)} %copy-done.1), kind=kLoop, calls=%fused_computation.1 | loop fusion | flops 802816 | bytes 2293760 | tf_op jit(solution)/shard_map/add | solution.py:417
  118.6 0.0 copy-done
  118.6 0.9 copy.9
Async XLA Ops:
  0.6 115.7 %copy-start.1 = (f32[112,1024]{1,0:T(8,128)S(1)}, f32[112,1024]{1,0:T(8,128)}, u32[]{:S(2)}) copy-start(f32[112,1024]{1,0:T(8,128)} %m1_ref.1) | copy-start | bytes 1376260
  0.6 115.7 %copy-start.2 = (f32[112,1024]{1,0:T(8,128)S(1)}, f32[112,1024]{1,0:T(8,128)}, u32[]{:S(2)}) copy-start(f32[112,1024]{1,0:T(8,128)} %m2_ref.1) | copy-start | bytes 1376260
  116.4 2.2 %copy-start = (bf16[4,112,1024]{2,1,0:T(8,128)(2,1)S(1)}, bf16[4,112,1024]{2,1,0:T(8,128)(2,1)}, u32[]{:S(2)}) copy-start(bf16[4,112,1024]{2,1,0:T(8,128)(2,1)} %get-tuple-element.6) | copy-start | bytes 2752516

commit v6 on v5

--- a/solution.py
+++ b/solution.py
@@ -23,7 +23,7 @@
 CHUNKS = 4
 WIDE = COLS // CHUNKS
 REACH = 8
-TILE = 512
+TILE = 1024
 
 
 def kernel(a_ref, b_ref, w_ref, m1_ref, m2_ref, grad_ref, wn_ref,
@@ -62,75 +62,6 @@
         copy.start()
     pl.semaphore_wait(barrier, len(near))
 
-    def number(up, e):
-        return 0 if e == REACH else RING - 1 if e == 0 else 1 + 2 * (REACH - 1 - e) + (0 if up else 1)
-
-    def pick(i, values):
-        return jnp.where(i == 0, values[0], jnp.where(i == 1, values[1], jnp.where(i == 2, values[2], values[3])))
-
-    turn = (y + 4 - 2 * c) % 4
-    owner = turn < 2
-    upward = jnp.logical_or(turn == 1, turn == 2)
-    side = turn % 2
-
-    def lanes(q):
-        return pl.ds(pl.multiple_of(q * PART, 128), PART)
-
-    def piece(n, q):
-        return at_all.at[n, :, lanes(q)]
-
-    def source(off, p, j):
-        k = ((4 * h + p + off + RING) % RING) // 4
-        return a_ref.at[pl.ds(pl.multiple_of(k * ROWS, 16), ROWS), lanes(j)]
-
-    home = [0, number(True, 4), number(False, 4), RING - 1]
-    offsets = [pick((l + 4 - y) % 4, v) for v in ([8, -7, 6, 7], [4, 5, -6, -5], [-4, -3, 2, 3], [0, 1, -2, -1])]
-
-    def scatter(i, j, stays):
-        q = 2 * c + j
-        return remote(source(offsets[i], y, j), piece(home[i], q) if stays else moved.at[y, i],
-                      sc_s.at[i, j], sc_r.at[y, i], dev(y_=q))
-
-    def stay(i):
-        return pltpu.make_async_copy(source(offsets[i], y, side), piece(home[i], y), stay_s.at[i])
-
-    for i in range(4):
-        for j in range(2):
-            @pl.when(jnp.logical_and(2 * c + j != y, y == l))
-            def _():
-                scatter(i, j, True).start()
-
-            @pl.when(jnp.logical_and(2 * c + j != y, y != l))
-            def _():
-                scatter(i, j, False).start()
-
-        @pl.when(jnp.logical_and(owner, y == l))
-        def _():
-            stay(i).start()
-
-    rank = {(1, 7): 0, (0, 7): 0, (1, 6): 0, (0, 6): 1, (1, 5): 1, (0, 5): 1,
-            (1, 3): 2, (0, 3): 2, (1, 2): 2, (0, 2): 3, (1, 1): 3, (0, 1): 3}
-
-    def z_move(src, n, p):
-        return remote(src, piece(n, y), zm_s.at[n], zm_r.at[n], dev(z_=4 * h + p))
-
-    def scattered(p, i):
-        return remote(moved.at[p, i], moved.at[p, i], sc_s.at[0, 0], sc_r.at[p, i], dev(c_=1 - c))
-
-    def z_moves(*which):
-        for up, e in which:
-            n = number(up, e)
-            p = (l + 8 - e) % 4 if up else (l + e) % 4
-
-            @pl.when(jnp.logical_and(owner, p == y))
-            def _():
-                z_move(source(e if up else -e, p, side), n, p).start()
-
-            @pl.when(jnp.logical_and(owner, p != y))
-            def _():
-                scattered(p, rank[up, e]).wait_recv()
-                z_move(moved.at[p, rank[up, e]], n, p).start()
-
     def b_move(q, half, up, slot):
         piece = pl.ds(half * (PART // 2), PART // 2)
         src = b_all.at[q, piece, :] if slot == 2 else b_ref.at[piece, :]
@@ -140,6 +71,75 @@
     for slot in (0, 1):
         for up in (1, 0):
             b_move(x, slot if up else 1 - slot, up, slot).start()
+
+    def number(up, e):
+        return 0 if e == REACH else RING - 1 if e == 0 else 1 + 2 * (REACH - 1 - e) + (0 if up else 1)
+
+    def pick(i, values):
+        return jnp.where(i == 0, values[0], jnp.where(i == 1, values[1], jnp.where(i == 2, values[2], values[3])))
+
+    turn = (y + 4 - 2 * c) % 4
+    owner = turn < 2
+    upward = jnp.logical_or(turn == 1, turn == 2)
+    side = turn % 2
+
+    def lanes(q):
+        return pl.ds(pl.multiple_of(q * PART, 128), PART)
+
+    def piece(n, q):
+        return at_all.at[n, :, lanes(q)]
+
+    def source(off, p, j):
+        k = ((4 * h + p + off + RING) % RING) // 4
+        return a_ref.at[pl.ds(pl.multiple_of(k * ROWS, 16), ROWS), lanes(j)]
+
+    home = [0, number(True, 4), number(False, 4), RING - 1]
+    offsets = [pick((l + 4 - y) % 4, v) for v in ([8, -7, 6, 7], [4, 5, -6, -5], [-4, -3, 2, 3], [0, 1, -2, -1])]
+
+    def scatter(i, j, stays):
+        q = 2 * c + j
+        return remote(source(offsets[i], y, j), piece(home[i], q) if stays else moved.at[y, i],
+                      sc_s.at[i, j], sc_r.at[y, i], dev(y_=q))
+
+    def stay(i):
+        return pltpu.make_async_copy(source(offsets[i], y, side), piece(home[i], y), stay_s.at[i])
+
+    for i in range(4):
+        for j in range(2):
+            @pl.when(jnp.logical_and(2 * c + j != y, y == l))
+            def _():
+                scatter(i, j, True).start()
+
+            @pl.when(jnp.logical_and(2 * c + j != y, y != l))
+            def _():
+                scatter(i, j, False).start()
+
+        @pl.when(jnp.logical_and(owner, y == l))
+        def _():
+            stay(i).start()
+
+    rank = {(1, 7): 0, (0, 7): 0, (1, 6): 0, (0, 6): 1, (1, 5): 1, (0, 5): 1,
+            (1, 3): 2, (0, 3): 2, (1, 2): 2, (0, 2): 3, (1, 1): 3, (0, 1): 3}
+
+    def z_move(src, n, p):
+        return remote(src, piece(n, y), zm_s.at[n], zm_r.at[n], dev(z_=4 * h + p))
+
+    def scattered(p, i):
+        return remote(moved.at[p, i], moved.at[p, i], sc_s.at[0, 0], sc_r.at[p, i], dev(c_=1 - c))
+
+    def z_moves(*which):
+        for up, e in which:
+            n = number(up, e)
+            p = (l + 8 - e) % 4 if up else (l + e) % 4
+
+            @pl.when(jnp.logical_and(owner, p == y))
+            def _():
+                z_move(source(e if up else -e, p, side), n, p).start()
+
+            @pl.when(jnp.logical_and(owner, p != y))
+            def _():
+                scattered(p, rank[up, e]).wait_recv()
+                z_move(moved.at[p, rank[up, e]], n, p).start()
 
     def to_up(n):
         return remote(piece(n, y), piece(n, y), up_y.at[n], nb_r.at[n], dev(y_=y_up))
@@ -241,10 +241,10 @@
     share(0)
     z_moves((1, 6), (0, 6), (1, 5), (0, 5))
     share(1, 2)
-    relay(0)
     for up, q in ((1, x_dn), (0, x_up)):
         b_move(q, 1 - up, up, 0).wait_recv()
         b_move(q, 1 - up, up, 2).start()
+    relay(0)
     share(3, 4)
     relay(1, 2)
     far(0)

time: 121 us -> 121 us (level)
  no operation moved by 1% of the time
where the time goes in v6:
time: 121 us; the launch traced here: 119 us
  Pallas kernels  115 us (95%)
  other arithmetic  2.22 us (2%)
    pallas_call x1, Pallas kernels, body(): pl.pallas_call(kernel, name='adam_grad', out_shape=(jax.ShapeDtypeStruct(...  115 us

profile of v6, /device:TPU:6, one launch (start us, length us, event | category | flops | bytes accessed | tf_op | source)
XLA Modules:
  0.0 119.2 jit_solution(1167161577278216384)
XLA Ops:
  0.6 0.0 copy-start.1
  0.6 0.0 copy-start.2
  0.7 115.3 %adam_grad.1 = (f32[112,1024]{1,0:T(8,128)}, bf16[4,112,1024]{2,1,0:T(8,128)(2,1)}) custom-call(bf16[448,768]{1,0:T(8,128)(2,1)} %bitcast.3, bf16[384,1024]{1,0:T(8,128)(2,1)} %b_ref.1, bf16[112,1024]{1,0:T(8,128)(2,1)} %w_ref.1, f32[112,1024]{1,0:T(8,128)} %m1_ref.1, f32[112,1024]{1,0:T(8,128)} %m2_ref.1), custom_call_target="tpu_custom_call" | custom-call | flops 5699999744 | bytes 6000000 | tf_op jit(solution)/shard_map/adam_grad/pallas_call | solution.py:387
  116.0 0.0 copy-done.1
  116.0 0.0 copy-done.2
  116.0 0.0 copy-start
  116.0 2.2 %fusion = (f32[112,1024]{1,0:T(8,128)}, f32[112,1024]{1,0:T(8,128)}) fusion(f32[112,1024]{1,0:T(8,128)} %get-tuple-element.5, f32[112,1024]{1,0:T(8,128)S(1)} %copy-done.2, f32[112,1024]{1,0:T(8,128)S(1)} %copy-done.1), kind=kLoop, calls=%fused_computation.1 | loop fusion | flops 802816 | bytes 2293760 | tf_op jit(solution)/shard_map/add | solution.py:417
  118.2 0.0 copy-done
  118.2 0.9 copy.9
Async XLA Ops:
  0.6 115.4 %copy-start.1 = (f32[112,1024]{1,0:T(8,128)S(1)}, f32[112,1024]{1,0:T(8,128)}, u32[]{:S(2)}) copy-start(f32[112,1024]{1,0:T(8,128)} %m1_ref.1) | copy-start | bytes 1376260
  0.6 115.4 %copy-start.2 = (f32[112,1024]{1,0:T(8,128)S(1)}, f32[112,1024]{1,0:T(8,128)}, u32[]{:S(2)}) copy-start(f32[112,1024]{1,0:T(8,128)} %m2_ref.1) | copy-start | bytes 1376260
  116.0 2.2 %copy-start = (bf16[4,112,1024]{2,1,0:T(8,128)(2,1)S(1)}, bf16[4,112,1024]{2,1,0:T(8,128)(2,1)}, u32[]{:S(2)}) copy-start(bf16[4,112,1024]{2,1,0:T(8,128)(2,1)} %get-tuple-element.6) | copy-start | bytes 2752516
